TPU v7x, 32 devices: a whole 2x2x4 slice. The times are simulated.
32 devices in a mesh: row: 8 (over y, x, core), col: 4 (over z).
Axes of the slice: x: 2, y: 2, z: 4, core: 2. Of those that a mesh axis runs over, the one named last changes fastest.
Arguments:
- probes: bfloat16 [8, 1024, 256], P('row', 'col'), may hold values from -6 to 6
- kernel_spectra: bfloat16 [2, 1024, 1024, 256], P(None, 'row', 'col'), may hold values from -0.25 to 0.25
- sensor_mask: int32 [1024], P('row'), may hold values 0 or 1
- precision: float32 [1024], P('row'), may hold values from 0.25 to 4
- source_block: int32 [1024], P('col'), may hold values from 0 to 15
- damping: float32 [16], replicated, may hold values from 0.2 to 2
Outputs:
- hessian_product: float32 [8, 1024, 256], P('row', 'col')
Inputs may be any that keep to these rules, and one draw needn't show every extreme that they name: `sensor_mask`: 1 marks a sensor whose records count. `source_block`: each entry names one of the 16 damping groups.
All inputs are finite; a program needn't handle non-finite values. No bound on the sum of `sensor_mask` on one device may be relied on, other than what follows from the above.
Results may differ from a plain program's by a relative error of at most 0.023.
Values may be sent and summed in bfloat16 or wider, within the bound.
A program may use at most 256 MiB of HBM per device.

v0:
```python
import math

import jax
import jax.numpy as jnp
from jax import lax
from jax.sharding import PartitionSpec as P


def dft_tables(length):
    period = 2 * length
    positions = jnp.arange(length, dtype=jnp.int32)
    phases = positions[:, None] * positions[None, :] % period
    angles = phases.astype(jnp.float32) * (2.0 * math.pi / period)
    cosine = jnp.cos(angles)
    sines = jnp.sin(angles)
    weight = jnp.where(positions == 0, 1.0, 2.0).astype(jnp.float32) / period
    forward = jnp.concatenate([cosine, -sines], axis=1).astype(jnp.bfloat16)
    inverse = jnp.concatenate([cosine * weight[:, None], -sines * weight[:, None]], axis=0).astype(
        jnp.bfloat16
    )
    return (forward, inverse)


def transform(block, table):
    dims_in = block.shape
    flattened = block.reshape(-1, dims_in[-1])
    result = jnp.dot(flattened, table, preferred_element_type=jnp.float32)
    return result.reshape(dims_in[:-1] + (table.shape[1],))


def freq_forward(real_pair, imag_pair, spectra):
    freq_count = real_pair.shape[3]
    split = spectra.reshape(spectra.shape[:-1] + (2, freq_count))
    out_real = jnp.einsum("krsf,pskf->prf", real_pair, split, preferred_element_type=jnp.float32)
    out_imag = jnp.einsum("krsf,pskf->prf", imag_pair, split, preferred_element_type=jnp.float32)
    joined = jnp.stack([out_real, out_imag], axis=-2)
    return joined.reshape(joined.shape[:-2] + (2 * freq_count,))


def freq_adjoint(real_pair, imag_pair, spectra):
    freq_count = real_pair.shape[3]
    split = spectra.reshape(spectra.shape[:-1] + (2, freq_count))
    g_real = jnp.einsum("krsf,prkf->psf", real_pair, split, preferred_element_type=jnp.float32)
    g_imag = jnp.einsum("krsf,prkf->psf", imag_pair, split, preferred_element_type=jnp.float32)
    joined = jnp.stack([g_real, g_imag], axis=-2)
    return joined.reshape(joined.shape[:-2] + (2 * freq_count,))


def body(probes, kernel_spectra, sensor_mask, precision, source_block, damping):
    forward, inverse = dft_tables(probes.shape[2])
    analysis = inverse.T
    synthesis = forward.T
    kernel_real = kernel_spectra[0]
    kernel_imag = kernel_spectra[1]
    negated_imag = -kernel_imag
    fwd_real = jnp.stack([kernel_real, negated_imag], axis=0)
    fwd_imag = jnp.stack([kernel_imag, kernel_real], axis=0)
    adj_imag = jnp.stack([negated_imag, kernel_real], axis=0)
    spectra = transform(lax.all_gather(probes, "row", axis=0, tiled=True), forward).astype(
        jnp.bfloat16
    )
    block_spec = freq_forward(fwd_real, fwd_imag, spectra).astype(jnp.bfloat16)
    pred_term = transform(block_spec, inverse)
    record_weight = jnp.where(sensor_mask == 1, precision, jnp.zeros_like(precision))
    predicted = lax.psum_scatter(
        pred_term.astype(jnp.bfloat16), "col", scatter_dimension=0, tiled=True
    ).astype(jnp.float32)
    weighted = (predicted * record_weight[None, :, None]).astype(jnp.bfloat16)
    residual_spec = transform(lax.all_gather(weighted, "col", axis=0, tiled=True), analysis).astype(
        jnp.bfloat16
    )
    block_grad = freq_adjoint(kernel_spectra, adj_imag, residual_spec).astype(jnp.bfloat16)
    summed = lax.psum_scatter(
        transform(block_grad, synthesis).astype(jnp.bfloat16),
        "row",
        scatter_dimension=0,
        tiled=True,
    ).astype(jnp.float32)
    groups = jnp.arange(damping.shape[0], dtype=jnp.int32)
    one_hot = (source_block[:, None] == groups[None, :]).astype(jnp.float32)
    source_damping = jnp.dot(one_hot, damping, precision=lax.Precision.HIGHEST)
    return summed + source_damping[None, :, None] * probes.astype(jnp.float32)


def solution(mesh):
    placed = (P("row", "col", None), P(None, "row", "col", None), P("row"), P("row"), P("col"), P())
    return jax.shard_map(
        body, mesh=mesh, in_specs=placed, out_specs=P("row", "col", None), check_vma=False
    )
```

profile of v0, /device:TPU:1, one launch (start us, length us, event | category | flops | bytes accessed | tf_op | source)
XLA Modules:
  0.0 272.5 jit_solution(7945707608915520706)
XLA Ops:
  6.5 0.7 all-gather.2.cloned.1.call-update
  7.3 0.0 reduce-scatter.3.cloned.1.call-start
  7.3 1.1 fusion.39
  8.4 45.0 %copy.15 = bf16[2,128,256,256]{2,1,0,3:T(8,128)(2,1)} copy(bf16[2,128,256,256]{3,2,1,0:T(8,128)(2,1)} %param.7) | data formatting | bytes 67108864 | tf_op args[1]
  53.4 27.1 %slice_negate_fusion = (bf16[1,128,256,256]{2,1,0,3:T(8,128)(2,1)}, bf16[1,128,256,256]{2,1,0,3:T(8,128)(2,1)}, bf16[1,128,256,256]{2,1,0,3:T(8,128)(2,1)}) fusion(bf16[2,128,256,256]{2,1,0,3:T(8,128)(2,1)} %copy.15), kind=kLoop, calls=%fused_computation.60 | loop fusion | flops 8388608 | bytes 83886080 | tf_op jit(solution)/shard_map/neg | solution.py:55
  80.5 1.1 multiply_convert_fusion.2
  81.6 44.3 %pad_maximum_fusion.3 = (bf16[2,128,256,256]{2,1,0,3:T(8,128)(2,1)}, bf16[2,128,256,256]{2,1,0,3:T(8,128)(2,1)}) fusion(bf16[1,128,256,256]{2,1,0,3:T(8,128)(2,1)} %get-tuple-element.5, bf16[1,128,256,256]{2,1,0,3:T(8,128)(2,1)} %get-tuple-element.7, bf16[1,128,256,256]{2,1,0,3:T(8,128)(2,1)} %get-tuple-element.6), kind=kLoop, calls=%fused_computation.3 | loop fusion | flops 33554432 | bytes 117440512 | tf_op jit(solution)/shard_map/stack | solution.py:56
  125.9 0.0 all-gather.2.cloned.1.call-done
  126.0 2.0 convolution_convert_fusion
  128.0 0.7 copy.30
  128.7 14.0 %fusion.25 = bf16[8,128,1,256]{1,0,3,2:T(8,128)(2,1)S(1)} fusion(bf16[8,256,2,256]{1,0,3,2:T(8,128)(2,1)S(1)} %bitcast.65, bf16[2,128,256,256]{2,1,0,3:T(8,128)(2,1)} %get-tuple-element.8), kind=kOutput, calls=%fused_computation.24 | convolution fusion | flops 268697600 | bytes 36175872 | tf_op jit(solution)/shard_map/krsf,pskf->prf/dot_general | solution.py:34
  142.6 0.0 copy-start.3
  142.7 14.0 %fusion.28 = bf16[8,128,1,256]{1,0,3,2:T(8,128)(2,1)S(1)} fusion(bf16[8,256,2,256]{1,0,3,2:T(8,128)(2,1)S(1)} %bitcast.66, bf16[2,128,256,256]{2,1,0,3:T(8,128)(2,1)} %get-tuple-element.9), kind=kOutput, calls=%fused_computation.25 | convolution fusion | flops 268697600 | bytes 36175872 | tf_op jit(solution)/shard_map/krsf,pskf->prf/dot_general | solution.py:35
  156.6 0.1 pad_maximum_fusion.9
  156.7 1.3 convolution_convert_fusion.2
  158.1 0.0 reduce-scatter.3.cloned.1.call-update
  158.1 0.0 reduce-scatter.5.cloned.1.call-start
  158.2 21.7 %reduce-scatter.3.cloned.1.call-done = bf16[2,128,256]{2,1,0:T(8,128)(2,1)} async-done(((bf16[8,128,256]{2,1,0:T(8,128)(2,1)}), bf16[2,128,256]{2,1,0:T(8,128)(2,1)}) %reduce-scatter.3.cloned.1.call-update) | async-done | bytes 131088 | tf_op jit(solution)/shard_map/reduce_scatter | solution.py:65
  179.9 1.0 multiply_convert_fusion
  180.9 13.3 %all_gather.7 = bf16[8,128,256]{2,1,0:T(8,128)(2,1)S(1)} all-gather(bf16[2,128,256]{2,1,0:T(8,128)(2,1)S(1)} %multiply_convert_fusion), channel_id=1, replica_groups=mesh['row'=8,'col'=4] {'col'}, dimensions={0}, use_global_device_ids=true | all-gather | bytes 655360 | tf_op jit(solution)/shard_map/all_gather | solution.py:69
  194.2 0.5 convolution_convert_fusion.1
  194.7 0.3 reshape.40
  195.0 1.7 copy.19
  196.7 13.0 %fusion.12 = bf16[8,256,1,256]{1,0,3,2:T(8,128)(2,1)S(1)} fusion(bf16[8,128,2,256]{1,0,2,3:T(8,128)(2,1)S(1)} %copy.19, bf16[1,128,256,256]{2,1,0,3:T(8,128)(2,1)} %get-tuple-element.7, bf16[1,128,256,256]{2,1,0,3:T(8,128)(2,1)} %get-tuple-element.5), kind=kOutput, calls=%fused_computation.18 | convolution fusion | flops 285736960 | bytes 35651584 | tf_op jit(solution)/shard_map/krsf,prkf->psf/dot_general | solution.py:44
  209.8 0.0 copy-start.2
  209.8 13.0 %fusion.11 = bf16[8,256,1,256]{1,0,3,2:T(8,128)(2,1)S(1)} fusion(bf16[8,128,2,256]{1,0,2,3:T(8,128)(2,1)S(1)} %copy.19, bf16[2,128,256,256]{2,1,0,3:T(8,128)(2,1)} %copy.15), kind=kOutput, calls=%fused_computation.17 | convolution fusion | flops 268959744 | bytes 35651584 | tf_op jit(solution)/shard_map/krsf,prkf->psf/dot_general | solution.py:43
  222.8 0.2 pad_maximum_fusion.4
  223.0 2.3 fusion.8
  225.4 0.0 reduce-scatter.5.cloned.1.call-update
  225.4 0.2 fusion.42
  225.6 38.7 %reduce-scatter.5.cloned.1.call-done = bf16[1,256,256]{2,1,0:T(8,128)(2,1)} async-done(((bf16[8,256,256]{2,1,0:T(8,128)(2,1)}), bf16[1,256,256]{2,1,0:T(8,128)(2,1)}) %reduce-scatter.5.cloned.1.call-update) | async-done | bytes 131088 | tf_op jit(solution)/shard_map/reduce_scatter | solution.py:73
  264.3 1.7 multiply_add_fusion
  (11 shorter events, 0.0 us)
Async XLA Ops:
  6.5 218.9 %copy-start = (f32[16]{0:T(128)S(1)}, f32[16]{0:T(128)}, u32[]{:S(2)}) copy-start(f32[16]{0:T(128)} %param.11) | copy-start | bytes 196
  6.5 119.4 %all-gather.2.cloned.1.call-start = ((), (), s32[]{:S(2)}) async-start(), calls=%async_computation.2 | async-start | bytes 1179648 | tf_op jit(solution)/shard_map/all_gather | solution.py:59
  7.3 172.6 %reduce-scatter.3.cloned.1.call-start = ((), (), s32[]{:S(2)}) async-start(), calls=%async_computation.3 | async-start | bytes 655360 | tf_op jit(solution)/shard_map/reduce_scatter | solution.py:65
  142.6 15.5 %copy-start.3 = (f32[128]{0:T(128)S(1)}, f32[128]{0:T(128)}, u32[]{:S(2)}) copy-start(f32[128]{0:T(128)} %param.9) | copy-start | bytes 1540
  142.6 15.5 %copy-start.4 = (s32[128]{0:T(128)S(1)}, s32[128]{0:T(128)}, u32[]{:S(2)}) copy-start(s32[128]{0:T(128)} %param.8) | copy-start | bytes 1540
  158.1 106.2 %reduce-scatter.5.cloned.1.call-start = ((), (), s32[]{:S(2)}) async-start(), calls=%async_computation.4 | async-start | bytes 1179648 | tf_op jit(solution)/shard_map/reduce_scatter | solution.py:73
  209.8 15.6 %copy-start.2 = (s32[256]{0:T(256)S(1)}, s32[256]{0:T(256)}, u32[]{:S(2)}) copy-start(s32[256]{0:T(256)} %param.10) | copy-start | bytes 3076
  209.8 54.5 %copy-start.1 = (bf16[1,256,256]{2,1,0:T(8,128)(2,1)S(1)}, bf16[1,256,256]{2,1,0:T(8,128)(2,1)}, u32[]{:S(2)}) copy-start(bf16[1,256,256]{2,1,0:T(8,128)(2,1)} %param.6) | copy-start | bytes 393220
Sparse Core Ops, SparseCore 0:
  9.2 25.9 all-gather.1
  158.2 21.6 reduce-scatter.2
  225.5 38.7 reduce-scatter.4
where the time goes:
time: 275 us; the launch traced here: 273 us
  other arithmetic  76.6 us (28%)
  waiting for transfers between devices  61.2 us (22%)
  matrix products  60.3 us (22%)
  local copies, waits for them, and re-layouts  47.7 us (17%)
  blocking collectives  13.3 us (5%)
  between operations  13.3 us (5%)
    unnamed x12, local copies, waits for them, and re-layouts  45.7 us
    another operation x1, other arithmetic, body(): fwd_real = jnp.stack([kernel_real, negated_imag], axis=0)  44.3 us
    reduce_scatter x1, waiting for transfers between devices, body(): lax.psum_scatter(transform(block_grad, synthesis).astype(jnp.bfloat16), '...  38.7 us
    neg x1, other arithmetic, body(): negated_imag = -kernel_imag  27.1 us
    reduce_scatter x1, waiting for transfers between devices, body(): lax.psum_scatter(pred_term.astype(jnp.bfloat16), 'col', scatter_dimension...  21.7 us
    dot_general x1, matrix products, freq_forward(): jnp.einsum('krsf,pskf->prf', imag_pair, split, preferred_element_type=jnp...  14 us
    dot_general x1, matrix products, freq_forward(): jnp.einsum('krsf,pskf->prf', real_pair, split, preferred_element_type=jnp...  14 us
    all_gather x1, blocking collectives, body(): lax.all_gather(weighted, 'col', axis=0, tiled=True)  13.3 us
  transfers between devices with their start and end apart: 3, of which 2 were waited for; matrix products, arithmetic and copies ran while one was open for 44% of the time, Pallas kernels for 0%

commit v1 on v0

v1 whole, which is shorter than its diff:
```python
import functools
import math

import jax
import jax.numpy as jnp
import ml_dtypes
import numpy as np
from jax import lax
from jax.experimental import pallas as pl
from jax.experimental.pallas import tpu as pltpu
from jax.sharding import PartitionSpec as P

GROUP = 16
NT = (((1,), (1,)), ((), ()))
TN = (((0,), (0,)), ((), ()))


def dft_tables(length):
    period = 2 * length
    positions = np.arange(length)
    phases = positions[:, None] * positions[None, :] % period
    angles = phases * (2.0 * math.pi / period)
    cosine = np.cos(angles).astype(np.float32)
    sines = np.sin(angles).astype(np.float32)
    weight = (np.where(positions == 0, 1.0, 2.0) / period).astype(np.float32)
    forward = np.concatenate([cosine, -sines], axis=1).astype(ml_dtypes.bfloat16)
    inverse = np.concatenate([cosine * weight[:, None], -sines * weight[:, None]], axis=0).astype(
        ml_dtypes.bfloat16
    )
    return (forward, inverse)


def dot(a, b, dims=None):
    if dims is None:
        return jnp.dot(a, b, preferred_element_type=jnp.float32)
    return lax.dot_general(a, b, dims, preferred_element_type=jnp.float32)


def forward_kernel(k_ref, probes_ref, fwd_t_ref, inv_t_ref, kt_ref, pred_ref, x_ref, e_ref):
    step = pl.program_id(0)
    _, rows, sources, freqs = k_ref.shape
    groups = freqs // GROUP
    nprobe = probes_ref.shape[0]
    columns = nprobe * 2 * GROUP

    @pl.when(step == 0)
    def _():
        for p in range(nprobe):
            spec = dot(fwd_t_ref[...], probes_ref[p], NT).astype(jnp.bfloat16)
            real = spec[:freqs].reshape(groups, GROUP, sources)
            imag = spec[freqs:].reshape(groups, GROUP, sources)
            at = p * 2 * GROUP
            x_ref[:, 0, at : at + GROUP, :] = real
            x_ref[:, 0, at + GROUP : at + 2 * GROUP, :] = imag
            x_ref[:, 1, at : at + GROUP, :] = -imag
            x_ref[:, 1, at + GROUP : at + 2 * GROUP, :] = real

    def turn(r, carry):
        for k in range(2):
            kt_ref[:, k, r, :, :] = k_ref[k, r].T.reshape(groups, GROUP, sources)
        return carry

    lax.fori_loop(0, rows, turn, 0, unroll=2)

    own = lax.broadcasted_iota(jnp.int32, (rows * GROUP, columns), 0) % GROUP
    col = lax.broadcasted_iota(jnp.int32, (rows * GROUP, columns), 1) % GROUP
    keep = own == col
    pick_row = lax.broadcasted_iota(jnp.int32, (rows, rows * GROUP), 0)
    pick_col = lax.broadcasted_iota(jnp.int32, (rows, rows * GROUP), 1) // GROUP
    pick = (pick_row == pick_col).astype(jnp.bfloat16)
    at_row = pl.ds(pl.multiple_of(step * rows, rows), rows)
    for g in range(groups):
        left = kt_ref[g].reshape(2, rows * GROUP, sources)
        out = dot(left[0], x_ref[g, 0], NT) + dot(left[1], x_ref[g, 1], NT)
        kept = jnp.where(keep, out, 0.0).astype(jnp.bfloat16)
        e_ref[at_row, g * columns : (g + 1) * columns] = dot(pick, kept).astype(jnp.bfloat16)

    @pl.when(step == pl.num_programs(0) - 1)
    def _():
        sensors = e_ref.shape[0]
        turned = e_ref[...].T.reshape(groups, nprobe, 2, GROUP, sensors)
        for p in range(nprobe):
            spec = jnp.concatenate(
                [turned[:, p, k].reshape(freqs, sensors) for k in range(2)], axis=0
            )
            pred_ref[p] = dot(inv_t_ref[...], spec).astype(jnp.bfloat16)


def adjoint_kernel(kt_ref, weighted_ref, inv_ref, syn_ref, out_ref, y_ref, g_ref):
    g = pl.program_id(0)
    sensors = weighted_ref.shape[2]
    nprobe = weighted_ref.shape[0]
    freqs = inv_ref.shape[0] // 2
    groups = freqs // GROUP
    sources = kt_ref.shape[-1]
    columns = nprobe * 2 * GROUP

    @pl.when(g == 0)
    def _():
        for p in range(nprobe):
            spec = dot(inv_ref[...], weighted_ref[p]).astype(jnp.bfloat16)
            for k in range(2):
                at = (2 * p + k) * GROUP
                y_ref[:, at : at + GROUP, :] = spec[k * freqs : (k + 1) * freqs].reshape(
                    groups, GROUP, sensors
                )

    part = 16
    width = part * GROUP
    own = lax.broadcasted_iota(jnp.int32, (columns, width), 0) % GROUP
    col = lax.broadcasted_iota(jnp.int32, (columns, width), 1) % GROUP
    keep = own == col
    spread_row = lax.broadcasted_iota(jnp.int32, (sensors, sensors * GROUP), 0)
    spread_col = lax.broadcasted_iota(jnp.int32, (sensors, sensors * GROUP), 1) // GROUP
    spread = (spread_row == spread_col).astype(jnp.bfloat16)
    y = y_ref[g]
    wide = []
    for n in range(sensors // part):
        piece = dot(y, spread[:, n * width : (n + 1) * width])
        wide.append(jnp.where(keep, piece, 0.0).astype(jnp.bfloat16))
    wide = jnp.concatenate(wide, axis=1)
    sums = [dot(wide, kt_ref[0, k].reshape(sensors * GROUP, sources)) for k in range(2)]
    real, imag = [s.reshape(nprobe, 2, GROUP, sources) for s in sums]
    at = pl.ds(pl.multiple_of(g * GROUP, GROUP), GROUP)
    late = pl.ds(pl.multiple_of(freqs + g * GROUP, GROUP), GROUP)
    g_ref[:, at, :] = (real[:, 0] + imag[:, 1]).astype(jnp.bfloat16)
    g_ref[:, late, :] = (real[:, 1] - imag[:, 0]).astype(jnp.bfloat16)

    @pl.when(g == pl.num_programs(0) - 1)
    def _():
        for p in range(nprobe):
            out_ref[p] = dot(g_ref[p], syn_ref[...], TN).astype(jnp.bfloat16)


def whole(shape):
    return pl.BlockSpec(shape, lambda i: (0,) * len(shape))


def forward_call(kernel_spectra, probes, fwd_t, inv_t):
    _, sensors, sources, freqs = kernel_spectra.shape
    nprobe, _, times = probes.shape
    groups = freqs // GROUP
    columns = nprobe * 2 * GROUP
    rows = 16
    return pl.pallas_call(
        forward_kernel,
        grid=(sensors // rows,),
        in_specs=[
            pl.BlockSpec((2, rows, sources, freqs), lambda i: (0, i, 0, 0)),
            whole(probes.shape),
            whole(fwd_t.shape),
            whole(inv_t.shape),
        ],
        out_specs=[
            pl.BlockSpec((groups, 2, rows, GROUP, sources), lambda i: (0, 0, i, 0, 0)),
            whole((nprobe, times, sensors)),
        ],
        out_shape=[
            jax.ShapeDtypeStruct((groups, 2, sensors, GROUP, sources), jnp.bfloat16),
            jax.ShapeDtypeStruct((nprobe, times, sensors), jnp.bfloat16),
        ],
        scratch_shapes=[
            pltpu.VMEM((groups, 2, columns, sources), jnp.bfloat16),
            pltpu.VMEM((sensors, groups * columns), jnp.bfloat16),
        ],
        compiler_params=pltpu.CompilerParams(vmem_limit_bytes=56 * 1024 * 1024),
        name="forward",
    )(kernel_spectra, probes, fwd_t, inv_t)


def adjoint_call(turned, weighted, inverse, synthesis):
    groups, _, sensors, _, sources = turned.shape
    nprobe, times, _ = weighted.shape
    freqs = groups * GROUP
    columns = nprobe * 2 * GROUP
    return pl.pallas_call(
        adjoint_kernel,
        grid=(groups,),
        in_specs=[
            pl.BlockSpec((1, 2, sensors, GROUP, sources), lambda i: (i, 0, 0, 0, 0)),
            whole(weighted.shape),
            whole(inverse.shape),
            whole(synthesis.shape),
        ],
        out_specs=whole((nprobe, sources, times)),
        out_shape=jax.ShapeDtypeStruct((nprobe, sources, times), jnp.bfloat16),
        scratch_shapes=[
            pltpu.VMEM((groups, columns, sensors), jnp.bfloat16),
            pltpu.VMEM((nprobe, 2 * freqs, sources), jnp.bfloat16),
        ],
        compiler_params=pltpu.CompilerParams(vmem_limit_bytes=56 * 1024 * 1024),
        name="adjoint",
    )(turned, weighted, inverse, synthesis)


def plain_forward(kernel_spectra, probes, fwd_t, inv_t):
    freqs = kernel_spectra.shape[3]
    spec = jnp.einsum("Ft,pst->psF", fwd_t, probes, preferred_element_type=jnp.float32)
    spec = spec.astype(jnp.bfloat16)
    spec = spec.reshape(spec.shape[:2] + (2, freqs))
    a = jnp.einsum("krsf,psjf->kjprf", kernel_spectra, spec, preferred_element_type=jnp.float32)
    both = jnp.concatenate([a[0, 0] - a[1, 1], a[0, 1] + a[1, 0]], axis=-1).astype(jnp.bfloat16)
    pred = jnp.einsum("tF,prF->ptr", inv_t, both, preferred_element_type=jnp.float32)
    return kernel_spectra, pred.astype(jnp.bfloat16)


def plain_adjoint(kernel_spectra, weighted, inverse, synthesis):
    freqs = kernel_spectra.shape[3]
    spec = jnp.einsum("Ft,ptr->prF", inverse, weighted, preferred_element_type=jnp.float32)
    spec = spec.astype(jnp.bfloat16)
    spec = spec.reshape(spec.shape[:2] + (2, freqs))
    a = jnp.einsum("krsf,prjf->kjpsf", kernel_spectra, spec, preferred_element_type=jnp.float32)
    both = jnp.concatenate([a[0, 0] + a[1, 1], a[0, 1] - a[1, 0]], axis=-1).astype(jnp.bfloat16)
    out = jnp.einsum("psF,Ft->pst", both, synthesis, preferred_element_type=jnp.float32)
    return out.astype(jnp.bfloat16)


def body(probes, kernel_spectra, sensor_mask, precision, source_block, damping):
    forward, inverse = dft_tables(probes.shape[2])
    fwd_t, inv_t = jnp.asarray(forward.T), jnp.asarray(inverse.T)
    inverse = jnp.asarray(inverse)
    _, sensors, sources, freqs = kernel_spectra.shape
    tiled = sensors % 128 == 0 and sources % 128 == 0 and freqs % 128 == 0
    run_forward = forward_call if tiled else plain_forward
    run_adjoint = adjoint_call if tiled else plain_adjoint

    gathered = lax.all_gather(probes, "row", axis=0, tiled=True)
    turned, pred = run_forward(kernel_spectra, gathered, fwd_t, inv_t)
    record_weight = jnp.where(sensor_mask == 1, precision, jnp.zeros_like(precision))
    predicted = lax.psum_scatter(pred, "col", scatter_dimension=0, tiled=True)
    weighted = (predicted.astype(jnp.float32) * record_weight[None, None, :]).astype(jnp.bfloat16)
    weighted = lax.all_gather(weighted, "col", axis=0, tiled=True)
    part = run_adjoint(turned, weighted, inverse, fwd_t)
    summed = lax.psum_scatter(part, "row", scatter_dimension=0, tiled=True).astype(jnp.float32)
    groups = jnp.arange(damping.shape[0], dtype=jnp.int32)
    one_hot = (source_block[:, None] == groups[None, :]).astype(jnp.float32)
    source_damping = jnp.dot(one_hot, damping, precision=lax.Precision.HIGHEST)
    return summed + source_damping[None, :, None] * probes.astype(jnp.float32)


def solution(mesh):
    placed = (P("row", "col", None), P(None, "row", "col", None), P("row"), P("row"), P("col"), P())
    return jax.shard_map(
        body, mesh=mesh, in_specs=placed, out_specs=P("row", "col", None), check_vma=False
    )
```

time: 275 us -> 194 us (0.71)
  Pallas kernels: 0 us -> 75.9 us
  other arithmetic: 76.6 us -> 2.65 us
  matrix products: 60.3 us -> 0.19 us
  local copies, waits for them, and re-layouts: 47.7 us -> 0.02 us
  waiting for transfers between devices: 61.2 us -> 87.6 us
    pallas_call x0 -> x2, Pallas kernels: none -> 75.9 us  [the longest x1 48.9 us: forward_call(): pl.pallas_call(forward_kernel, grid=(sensors // rows,), in_specs=[pl.Bloc...]
    dot_general x8 -> x0, matrix products: 60.1 us -> none  [the longest x1 14 us: freq_forward(): jnp.einsum('krsf,pskf->prf', imag_pair, split, preferred_element_type=jnp...]
    another operation x5 -> x0, other arithmetic: 46.8 us -> none  [the longest x1 44.3 us: body(): fwd_real = jnp.stack([kernel_real, negated_imag], axis=0)]
    unnamed x12 -> x10, local copies, waits for them, and re-layouts: 45.7 us -> 0.02 us
    all_gather x1, waiting for transfers between devices: 0.02 us -> 28 us  [body(): gathered = lax.all_gather(probes, 'row', axis=0, tiled=True)]
    neg x1 -> x0, other arithmetic: 27.1 us -> none  [body(): negated_imag = -kernel_imag]
  transfers between devices with their start and end apart: 3 -> 3, of which waited for: 2 -> 3; matrix products, arithmetic and copies ran while one was open for 44% -> 0% of each run, Pallas kernels for 0% -> 0%
where the time goes in v1:
time: 194 us; the launch traced here: 193 us
  waiting for transfers between devices  87.6 us (45%)
  Pallas kernels  75.9 us (39%)
  blocking collectives  13.3 us (7%)
  between operations  13.2 us (7%)
  other arithmetic  2.65 us (1%)
    pallas_call x1, Pallas kernels, forward_call(): pl.pallas_call(forward_kernel, grid=(sensors // rows,), in_specs=[pl.Bloc...  48.9 us
    reduce_scatter x1, waiting for transfers between devices, body(): lax.psum_scatter(part, 'row', scatter_dimension=0, tiled=True)  39.3 us
    all_gather x1, waiting for transfers between devices, body(): gathered = lax.all_gather(probes, 'row', axis=0, tiled=True)  28 us
    pallas_call x1, Pallas kernels, adjoint_call(): pl.pallas_call(adjoint_kernel, grid=(groups,), in_specs=[pl.BlockSpec((1,...  27 us
    reduce_scatter x1, waiting for transfers between devices, body(): predicted = lax.psum_scatter(pred, 'col', scatter_dimension=0, tiled=True)  19.6 us
    all_gather x1, blocking collectives, body(): weighted = lax.all_gather(weighted, 'col', axis=0, tiled=True)  13.3 us
  transfers between devices with their start and end apart: 3, of which 3 were waited for; matrix products, arithmetic and copies ran while one was open for 0% of the time, Pallas kernels for 0%

profile of v1, /device:TPU:1, one launch (start us, length us, event | category | flops | bytes accessed | tf_op | source)
XLA Modules:
  0.0 192.8 jit_solution(8716085312312121521)
XLA Ops:
  6.5 0.0 copy-start
  6.5 0.0 copy-start.4
  6.5 0.0 copy-start.3
  6.5 0.0 all-gather.2.cloned.1.call-start
  6.5 0.7 all-gather.2.cloned.1.call-update
  7.3 0.0 copy-start.2
  7.3 0.0 copy-start.1
  7.3 0.0 reduce-scatter.3.cloned.1.call-start
  7.3 28.0 %all-gather.2.cloned.1.call-done.probes_ref = bf16[8,256,256]{2,1,0:T(8,128)(2,1)} async-done(((bf16[1,256,256]{2,1,0:T(8,128)(2,1)}), bf16[8,256,256]{2,1,0:T(8,128)(2,1)}) %all-gather.2.cloned.1.call-update) | async-done | bytes 1048592 | tf_op jit(solution)/shard_map/all_gather | solution.py:227
  35.3 48.9 %forward.1 = (bf16[16,2,128,16,256]{4,3,2,1,0:T(8,128)(2,1)}, bf16[8,256,128]{2,1,0:T(8,128)(2,1)}) custom-call(bf16[2,128,256,256]{3,2,1,0:T(8,128)(2,1)} %k_ref.1, bf16[8,256,256]{2,1,0:T(8,128)(2,1)} %all-gather.2.cloned.1.call-done.probes_ref, bf16[512,256]{1,0:T(8,128)(2,1)} %constant.10.clone.fwd_t_ref.syn_ref, bf16[256,512]{1,0:T(8,128)(2,1)} %constant.11.clone.inv_t_ref), custom_call_target="tpu_custom_call" | custom-call | tf_op jit(solution)/shard_map/forward/pallas_call | solution.py:145
  84.2 0.0 reduce-scatter.3.cloned.1.call-update
  84.2 0.0 reduce-scatter.5.cloned.1.call-start
  84.3 0.0 copy-done.4
  84.3 0.0 copy-done.3
  84.3 19.6 %reduce-scatter.3.cloned.1.call-done = bf16[2,256,128]{2,1,0:T(8,128)(2,1)} async-done(((bf16[8,256,128]{2,1,0:T(8,128)(2,1)}), bf16[2,256,128]{2,1,0:T(8,128)(2,1)}) %reduce-scatter.3.cloned.1.call-update) | async-done | bytes 131088 | tf_op jit(solution)/shard_map/reduce_scatter | solution.py:230
  103.9 0.9 multiply_convert_fusion
  104.8 13.3 %all_gather.7.weighted_ref = bf16[8,256,128]{2,1,0:T(8,128)(2,1)} all-gather(bf16[2,256,128]{2,1,0:T(8,128)(2,1)S(1)} %multiply_convert_fusion), channel_id=1, replica_groups=mesh['row'=8,'col'=4] {'col'}, dimensions={0}, use_global_device_ids=true | all-gather | bytes 655360 | tf_op jit(solution)/shard_map/all_gather | solution.py:232
  118.1 27.0 %adjoint.1 = bf16[8,256,256]{2,1,0:T(8,128)(2,1)} custom-call(bf16[16,2,128,16,256]{4,3,2,1,0:T(8,128)(2,1)} %get-tuple-element.7.kt_ref, bf16[8,256,128]{2,1,0:T(8,128)(2,1)} %all_gather.7.weighted_ref, bf16[512,256]{1,0:T(8,128)(2,1)} %constant.12.clone.inv_ref, bf16[512,256]{1,0:T(8,128)(2,1)} %constant.10.clone.fwd_t_ref.syn_ref), custom_call_target="tpu_custom_call" | custom-call | tf_op jit(solution)/shard_map/adjoint/pallas_call | solution.py:176
  145.0 0.0 reduce-scatter.5.cloned.1.call-update
  145.1 0.0 copy-done
  145.1 0.0 copy-done.2
  145.1 0.2 fusion
  145.3 39.3 %reduce-scatter.5.cloned.1.call-done = bf16[1,256,256]{2,1,0:T(8,128)(2,1)} async-done(((bf16[8,256,256]{2,1,0:T(8,128)(2,1)}), bf16[1,256,256]{2,1,0:T(8,128)(2,1)}) %reduce-scatter.5.cloned.1.call-update) | async-done | bytes 131088 | tf_op jit(solution)/shard_map/reduce_scatter | solution.py:234
  184.6 0.0 copy-done.1
  184.6 1.7 multiply_add_fusion
  (1 shorter events, 0.0 us)
Async XLA Ops:
  6.5 138.5 %copy-start = (f32[16]{0:T(128)S(1)}, f32[16]{0:T(128)}, u32[]{:S(2)}) copy-start(f32[16]{0:T(128)} %param.14) | copy-start | bytes 196
  6.5 77.7 %copy-start.4 = (s32[128]{0:T(128)S(1)}, s32[128]{0:T(128)}, u32[]{:S(2)}) copy-start(s32[128]{0:T(128)} %param.11) | copy-start | bytes 1540
  6.5 77.7 %copy-start.3 = (f32[128]{0:T(128)S(1)}, f32[128]{0:T(128)}, u32[]{:S(2)}) copy-start(f32[128]{0:T(128)} %param.12) | copy-start | bytes 1540
  6.5 28.8 %all-gather.2.cloned.1.call-start = ((), (), s32[]{:S(2)}) async-start(), calls=%async_computation.2 | async-start | bytes 1179648 | tf_op jit(solution)/shard_map/all_gather | solution.py:227
  7.3 137.8 %copy-start.2 = (s32[256]{0:T(256)S(1)}, s32[256]{0:T(256)}, u32[]{:S(2)}) copy-start(s32[256]{0:T(256)} %param.13) | copy-start | bytes 3076
  7.3 177.3 %copy-start.1 = (bf16[1,256,256]{2,1,0:T(8,128)(2,1)S(1)}, bf16[1,256,256]{2,1,0:T(8,128)(2,1)}, u32[]{:S(2)}) copy-start(bf16[1,256,256]{2,1,0:T(8,128)(2,1)} %param.9) | copy-start | bytes 393220
  7.3 96.6 %reduce-scatter.3.cloned.1.call-start = ((), (), s32[]{:S(2)}) async-start(), calls=%async_computation.3 | async-start | bytes 655360 | tf_op jit(solution)/shard_map/reduce_scatter | solution.py:230
  84.2 100.4 %reduce-scatter.5.cloned.1.call-start = ((), (), s32[]{:S(2)}) async-start(), calls=%async_computation.4 | async-start | bytes 1179648 | tf_op jit(solution)/shard_map/reduce_scatter | solution.py:234
Sparse Core Ops, SparseCore 0:
  9.3 25.9 all-gather.1
  84.3 19.4 reduce-scatter.2
  145.2 39.3 reduce-scatter.4

commit v2 on v0

v2 whole, which is shorter than its diff:
```python
import functools
import math

import jax
import jax.numpy as jnp
import ml_dtypes
import numpy as np
from jax import lax
from jax.experimental import pallas as pl
from jax.experimental.pallas import tpu as pltpu
from jax.sharding import PartitionSpec as P

GROUP = 16
HALVES = 2
MESH = pl.DeviceIdType.MESH
NT = (((1,), (1,)), ((), ()))
TN = (((0,), (0,)), ((), ()))


def dft_tables(length):
    period = 2 * length
    positions = np.arange(length)
    phases = positions[:, None] * positions[None, :] % period
    angles = phases * (2.0 * math.pi / period)
    cosine = np.cos(angles).astype(np.float32)
    sines = np.sin(angles).astype(np.float32)
    weight = (np.where(positions == 0, 1.0, 2.0) / period).astype(np.float32)
    forward = np.concatenate([cosine, -sines], axis=1).astype(ml_dtypes.bfloat16)
    inverse = np.concatenate([cosine * weight[:, None], -sines * weight[:, None]], axis=0).astype(
        ml_dtypes.bfloat16
    )
    return (forward, inverse)


def dot(a, b, dims=None):
    if dims is None:
        return jnp.dot(a, b, preferred_element_type=jnp.float32)
    return lax.dot_general(a, b, dims, preferred_element_type=jnp.float32)


def fused_kernel(
    n_row,
    n_col,
    halves,
    k_hbm,
    probes_ref,
    weight_ref,
    fwd_t_ref,
    inv_ref,
    pick_ref,
    out_ref,
    stage,
    kt_ref,
    gath,
    x_ref,
    et_ref,
    pred_ref,
    pred_in,
    wt_ref,
    y_ref,
    acc_ref,
    g_ref,
    hess_out,
    hess_in,
    k_sem,
    gs_sem,
    gr_sem,
    ps_sem,
    pr_sem,
    ws_sem,
    wr_sem,
    hs_sem,
    hr_sem,
):
    me_row, me_col = lax.axis_index("row"), lax.axis_index("col")
    _, sensors, sources, freqs = k_hbm.shape
    nloc = probes_ref.shape[0]
    nprobe = nloc * n_row
    nown = nprobe // n_col
    groups = freqs // GROUP
    columns = nprobe * 2 * GROUP
    rows = stage.shape[2]
    steps = sensors // rows
    half = sensors // halves

    def row_peer(d):
        return lax.rem(me_row + d, n_row)

    def col_peer(d):
        return lax.rem(me_col + d, n_col)

    def load(step, slot):
        at = pl.ds(pl.multiple_of(step * rows, rows), rows)
        return pltpu.make_async_copy(k_hbm.at[:, at], stage.at[slot], k_sem.at[slot])

    for slot in range(2):
        load(slot, slot).start()

    barrier = pltpu.get_barrier_semaphore()
    for d in range(1, n_row):
        pl.semaphore_signal(barrier, inc=1, device_id=(row_peer(d), me_col), device_id_type=MESH)
    for d in range(1, n_col):
        pl.semaphore_signal(barrier, inc=1, device_id=(me_row, col_peer(d)), device_id_type=MESH)
    pl.semaphore_wait(barrier, n_row + n_col - 2)

    def send(src, dst, send_sem, recv_sem, device):
        return pltpu.make_async_remote_copy(
            src_ref=src,
            dst_ref=dst,
            send_sem=send_sem,
            recv_sem=recv_sem,
            device_id=device,
            device_id_type=MESH,
        )

    gathers = []
    for d in range(1, n_row):
        copy = send(
            probes_ref,
            gath.at[d],
            gs_sem.at[d],
            gr_sem.at[d],
            (row_peer(d), me_col),
        )
        copy.start()
        gathers.append(copy)

    def turn_step(step, carry):
        slot = lax.rem(step, 2)
        load(step, slot).wait()

        def turn(r, inner):
            for k in range(2):
                kt_ref[:, k, step * rows + r, :, :] = stage[slot, k, r].T.reshape(
                    groups, GROUP, sources
                )
            return inner

        lax.fori_loop(0, rows, turn, 0, unroll=2)

        @pl.when(step + 2 < steps)
        def _():
            load(step + 2, slot).start()

        return carry

    lax.fori_loop(0, steps, turn_step, 0)

    def spectra(p, block):
        spec = dot(fwd_t_ref[...], block, NT).astype(jnp.bfloat16)
        real = spec[:freqs].reshape(groups, GROUP, sources)
        imag = spec[freqs:].reshape(groups, GROUP, sources)
        first = pl.ds(pl.multiple_of(p * 2 * GROUP, GROUP), GROUP)
        second = pl.ds(pl.multiple_of(p * 2 * GROUP + GROUP, GROUP), GROUP)
        x_ref[:, 0, first, :] = real
        x_ref[:, 0, second, :] = imag
        x_ref[:, 1, first, :] = -imag
        x_ref[:, 1, second, :] = real

    for j in range(nloc):
        spectra(me_row * nloc + j, probes_ref[j])
    for d in range(1, n_row):
        gathers[d - 1].wait_recv()
        origin = lax.rem(me_row + n_row - d, n_row)
        for j in range(nloc):
            spectra(origin * nloc + j, gath[d, j])

    own = lax.broadcasted_iota(jnp.int32, (1, GROUP, columns), 1)
    col = lax.broadcasted_iota(jnp.int32, (1, GROUP, columns), 2) % GROUP
    keep = own == col
    own = lax.broadcasted_iota(jnp.int32, (1, GROUP, half * GROUP), 1)
    col = lax.broadcasted_iota(jnp.int32, (1, GROUP, half * GROUP), 2) % GROUP
    keep_wide = own == col

    def forward_part(h, low, high):
        def one(g, carry):
            left = [
                kt_ref[g, k, h * half : (h + 1) * half].reshape(half * GROUP, sources)
                for k in range(2)
            ]
            out = dot(left[0], x_ref[g, 0], NT) + dot(left[1], x_ref[g, 1], NT)
            kept = jnp.where(keep, out.reshape(half, GROUP, columns), 0.0).astype(jnp.bfloat16)
            block = dot(pick_ref[...], kept.reshape(half * GROUP, columns))
            et_ref[:, :, g] = (
                block.T.astype(jnp.bfloat16).reshape(nprobe, 2, GROUP, half)
            )
            return carry

        lax.fori_loop(low, high, one, 0)

    sends = []

    def predict(h):
        for p in range(nprobe):
            spec = et_ref[p].reshape(2 * freqs, half)
            pred_ref[h, p // nown, p % nown] = dot(spec, inv_ref[...], TN).astype(jnp.bfloat16)
        copies = []
        for d in range(1, n_col):
            copy = send(
                pred_ref.at[h, col_peer(d)],
                pred_in.at[h, d - 1],
                ps_sem.at[h, d - 1],
                pr_sem.at[h, d - 1],
                (me_row, col_peer(d)),
            )
            copy.start()
            copies.append(copy)
        sends.extend(copies)
        return copies

    def weigh(h, copies):
        total = pred_ref[h, me_col].astype(jnp.float32)
        for d in range(1, n_col):
            copies[d - 1].wait_recv()
            total = total + pred_in[h, d - 1].astype(jnp.float32)
        scale = weight_ref[h * half : (h + 1) * half, :]
        wt_ref[h, me_col] = (total * scale[None]).astype(jnp.bfloat16)
        out = []
        for d in range(1, n_col):
            copy = send(
                wt_ref.at[h, me_col],
                wt_ref.at[h, me_col],
                ws_sem.at[h, d - 1],
                wr_sem.at[h, d - 1],
                (me_row, col_peer(d)),
            )
            copy.start()
            out.append(copy)
        sends.extend(out)
        return out

    def residual(h, copies):
        for copy in copies:
            copy.wait_recv()
        for p in range(nprobe):
            spec = dot(inv_ref[...], wt_ref[h, p // nown, p % nown], NT).astype(jnp.bfloat16)
            for k in range(2):
                at = (2 * p + k) * GROUP
                y_ref[:, at : at + GROUP, :] = spec[k * freqs : (k + 1) * freqs].reshape(
                    groups, GROUP, half
                )

    def adjoint_part(h, low, high):
        def one(g, carry):
            wide = dot(y_ref[g], pick_ref[...]).reshape(2 * nprobe, GROUP, half * GROUP)
            wide = jnp.where(keep_wide, wide, 0.0).astype(jnp.bfloat16)
            wide = wide.reshape(columns, half * GROUP)
            both = [
                dot(
                    wide, kt_ref[g, k, h * half : (h + 1) * half].reshape(half * GROUP, sources)
                ).reshape(nprobe, 2, GROUP, sources)
                for k in range(2)
            ]
            real = both[0][:, 0] + both[1][:, 1]
            imag = both[0][:, 1] - both[1][:, 0]
            if h > 0:
                real = real + acc_ref[g, 0]
                imag = imag + acc_ref[g, 1]
            if h < halves - 1:
                acc_ref[g, 0] = real
                acc_ref[g, 1] = imag
            else:
                g_ref[:, 0, g] = real.astype(jnp.bfloat16)
                g_ref[:, 1, g] = imag.astype(jnp.bfloat16)
            return carry

        lax.fori_loop(low, high, one, 0)

    mid = groups // 2
    forward_part(0, 0, groups)
    pred_copies = predict(0)
    for h in range(1, halves):
        forward_part(h, 0, mid)
        wt_copies = weigh(h - 1, pred_copies)
        forward_part(h, mid, groups)
        pred_copies = predict(h)
        residual(h - 1, wt_copies)
        adjoint_part(h - 1, 0, mid)
        wt_copies = weigh(h, pred_copies)
        adjoint_part(h - 1, mid, groups)
    if halves == 1:
        wt_copies = weigh(0, pred_copies)
    residual(halves - 1, wt_copies)
    adjoint_part(halves - 1, 0, groups)

    def history(p):
        return dot(g_ref[p].reshape(2 * freqs, sources), fwd_t_ref[...], TN).astype(jnp.bfloat16)

    backs = []
    for d in range(1, n_row):
        peer = row_peer(d)
        for j in range(nloc):
            hess_out[d - 1, j] = history(peer * nloc + j)
        copy = send(
            hess_out.at[d - 1],
            hess_in.at[d - 1],
            hs_sem.at[d - 1],
            hr_sem.at[d - 1],
            (peer, me_col),
        )
        copy.start()
        backs.append(copy)
    for j in range(nloc):
        total = history(me_row * nloc + j).astype(jnp.float32)
        out_ref[j] = total
    for d in range(1, n_row):
        backs[d - 1].wait_recv()
        for j in range(nloc):
            out_ref[j] += hess_in[d - 1, j].astype(jnp.float32)
    for copy in gathers + sends + backs:
        copy.wait_send()


def fused_call(mesh_sizes, kernel_spectra, probes, weight, fwd_t, inverse):
    n_row, n_col = mesh_sizes
    _, sensors, sources, freqs = kernel_spectra.shape
    nloc, _, times = probes.shape
    nprobe = nloc * n_row
    nown = nprobe // n_col
    groups = freqs // GROUP
    columns = nprobe * 2 * GROUP
    halves = HALVES
    half = sensors // halves
    rows = 16
    owner = np.arange(half * GROUP)[None, :] // GROUP
    pick = jnp.asarray((np.arange(half)[:, None] == owner).astype(ml_dtypes.bfloat16))
    vmem = pl.BlockSpec(memory_space=pltpu.VMEM)
    low = jnp.bfloat16
    dma = pltpu.SemaphoreType.DMA
    return pl.pallas_call(
        functools.partial(fused_kernel, n_row, n_col, halves),
        in_specs=[pl.BlockSpec(memory_space=pl.ANY)] + [vmem] * 5,
        out_specs=vmem,
        out_shape=jax.ShapeDtypeStruct(probes.shape, jnp.float32),
        scratch_shapes=[
            pltpu.VMEM((2, 2, rows, sources, freqs), low),
            pltpu.VMEM((groups, 2, sensors, GROUP, sources), low),
            pltpu.VMEM((n_row,) + probes.shape, low),
            pltpu.VMEM((groups, 2, columns, sources), low),
            pltpu.VMEM((nprobe, 2, groups, GROUP, half), low),
            pltpu.VMEM((halves, n_col, nown, half, times), low),
            pltpu.VMEM((halves, n_col - 1, nown, half, times), low),
            pltpu.VMEM((halves, n_col, nown, half, times), low),
            pltpu.VMEM((groups, columns, half), low),
            pltpu.VMEM((groups, 2, nprobe, GROUP, sources), jnp.float32),
            pltpu.VMEM((nprobe, 2, groups, GROUP, sources), low),
            pltpu.VMEM((n_row - 1,) + probes.shape, low),
            pltpu.VMEM((n_row - 1,) + probes.shape, low),
            dma((2,)),
            dma((n_row,)),
            dma((n_row,)),
            dma((halves, n_col - 1)),
            dma((halves, n_col - 1)),
            dma((halves, n_col - 1)),
            dma((halves, n_col - 1)),
            dma((n_row - 1,)),
            dma((n_row - 1,)),
        ],
        compiler_params=pltpu.CompilerParams(
            vmem_limit_bytes=60 * 1024 * 1024, collective_id=0, has_side_effects=True
        ),
        name="fused",
    )(kernel_spectra, probes, weight, fwd_t, inverse, pick)


def plain_forward(kernel_spectra, probes, fwd_t, inv_t):
    freqs = kernel_spectra.shape[3]
    spec = jnp.einsum("Ft,pst->psF", fwd_t, probes, preferred_element_type=jnp.float32)
    spec = spec.astype(jnp.bfloat16)
    spec = spec.reshape(spec.shape[:2] + (2, freqs))
    a = jnp.einsum("krsf,psjf->kjprf", kernel_spectra, spec, preferred_element_type=jnp.float32)
    both = jnp.concatenate([a[0, 0] - a[1, 1], a[0, 1] + a[1, 0]], axis=-1).astype(jnp.bfloat16)
    pred = jnp.einsum("tF,prF->ptr", inv_t, both, preferred_element_type=jnp.float32)
    return kernel_spectra, pred.astype(jnp.bfloat16)


def plain_adjoint(kernel_spectra, weighted, inverse, synthesis):
    freqs = kernel_spectra.shape[3]
    spec = jnp.einsum("Ft,ptr->prF", inverse, weighted, preferred_element_type=jnp.float32)
    spec = spec.astype(jnp.bfloat16)
    spec = spec.reshape(spec.shape[:2] + (2, freqs))
    a = jnp.einsum("krsf,prjf->kjpsf", kernel_spectra, spec, preferred_element_type=jnp.float32)
    both = jnp.concatenate([a[0, 0] + a[1, 1], a[0, 1] - a[1, 0]], axis=-1).astype(jnp.bfloat16)
    out = jnp.einsum("psF,Ft->pst", both, synthesis, preferred_element_type=jnp.float32)
    return out.astype(jnp.bfloat16)


def plain(kernel_spectra, probes, record_weight, fwd_t, inverse):
    gathered = lax.all_gather(probes, "row", axis=0, tiled=True)
    turned, pred = plain_forward(kernel_spectra, gathered, fwd_t, inverse.T)
    predicted = lax.psum_scatter(pred, "col", scatter_dimension=0, tiled=True)
    weighted = (predicted.astype(jnp.float32) * record_weight[None, None, :]).astype(jnp.bfloat16)
    weighted = lax.all_gather(weighted, "col", axis=0, tiled=True)
    part = plain_adjoint(turned, weighted, inverse, fwd_t)
    return lax.psum_scatter(part, "row", scatter_dimension=0, tiled=True).astype(jnp.float32)


def body(sizes, probes, kernel_spectra, sensor_mask, precision, source_block, damping):
    forward, inverse = dft_tables(probes.shape[2])
    fwd_t, inverse = jnp.asarray(forward.T), jnp.asarray(inverse)
    _, sensors, sources, freqs = kernel_spectra.shape
    record_weight = jnp.where(sensor_mask == 1, precision, jnp.zeros_like(precision))
    if sensors % 128 == 0 and sources % 128 == 0 and freqs % 128 == 0:
        summed = fused_call(sizes, kernel_spectra, probes, record_weight[:, None], fwd_t, inverse)
    else:
        summed = plain(kernel_spectra, probes, record_weight, fwd_t, inverse)
    groups = jnp.arange(damping.shape[0], dtype=jnp.int32)
    one_hot = (source_block[:, None] == groups[None, :]).astype(jnp.float32)
    source_damping = jnp.dot(one_hot, damping, precision=lax.Precision.HIGHEST)
    return summed + source_damping[None, :, None] * probes.astype(jnp.float32)


def solution(mesh):
    placed = (P("row", "col", None), P(None, "row", "col", None), P("row"), P("row"), P("col"), P())
    sizes = (mesh.shape["row"], mesh.shape["col"])
    return jax.shard_map(
        functools.partial(body, sizes),
        mesh=mesh,
        in_specs=placed,
        out_specs=P("row", "col", None),
        check_vma=False,
    )
```

time: 275 us -> 96 us (0.35)
  Pallas kernels: 0 us -> 92.1 us
  other arithmetic: 76.6 us -> 2.55 us
  waiting for transfers between devices: 61.2 us -> 0 us
  matrix products: 60.3 us -> 0.19 us
  local copies, waits for them, and re-layouts: 47.7 us -> 0.75 us
  blocking collectives: 13.3 us -> 0 us
  between operations: 13.3 us -> 0.03 us
    pallas_call x0 -> x1, Pallas kernels: none -> 92.1 us  [fused_call(): pl.pallas_call(functools.partial(fused_kernel, n_row, n_col, halves), in_...]
    reduce_scatter x2 -> x0, waiting for transfers between devices: 60.4 us -> none  [the longest x1 38.7 us: body(): lax.psum_scatter(transform(block_grad, synthesis).astype(jnp.bfloat16), '...]
    dot_general x8 -> x0, matrix products: 60.1 us -> none  [the longest x1 14 us: freq_forward(): jnp.einsum('krsf,pskf->prf', imag_pair, split, preferred_element_type=jnp...]
    another operation x5 -> x0, other arithmetic: 46.8 us -> none  [the longest x1 44.3 us: body(): fwd_real = jnp.stack([kernel_real, negated_imag], axis=0)]
    unnamed x12 -> x6, local copies, waits for them, and re-layouts: 45.7 us -> 0.01 us
    neg x1 -> x0, other arithmetic: 27.1 us -> none  [body(): negated_imag = -kernel_imag]
    all_gather x1 -> x0, blocking collectives: 13.3 us -> none  [body(): lax.all_gather(weighted, 'col', axis=0, tiled=True)]
  transfers between devices with their start and end apart: 3 -> 0, of which waited for: 2 -> 0; matrix products, arithmetic and copies ran while one was open for 44% -> 0% of each run, Pallas kernels for 0% -> 0%
where the time goes in v2:
time: 96 us; the launch traced here: 95.6 us
  Pallas kernels  92.1 us (96%)
  other arithmetic  2.55 us (3%)
    pallas_call x1, Pallas kernels, fused_call(): pl.pallas_call(functools.partial(fused_kernel, n_row, n_col, halves), in_...  92.1 us

profile of v2, /device:TPU:1, one launch (start us, length us, event | category | flops | bytes accessed | tf_op | source)
XLA Modules:
  0.0 95.6 jit_solution(13372956997266078619)
XLA Ops:
  0.0 0.0 copy-start
  0.0 0.0 copy-start.1
  0.0 0.0 copy-start.2
  0.0 0.7 fusion.2
  0.7 0.7 copy.10.weight_ref
  1.5 92.1 %fused.1 = f32[1,256,256]{2,1,0:T(8,128)} custom-call(bf16[2,128,256,256]{3,2,1,0:T(8,128)(2,1)} %k_hbm.1, bf16[1,256,256]{2,1,0:T(8,128)(2,1)} %probes_ref.1, f32[128,1]{1,0:T(8,128)} %copy.10.weight_ref, bf16[512,256]{1,0:T(8,128)(2,1)} %constant.10.clone.fwd_t_ref, bf16[512,256]{1,0:T(8,128)(2,1)} %constant.11.clone.inv_ref, ...), custom_call_target="tpu_custom_call" | custom-call | tf_op jit(solution)/shard_map/fused/pallas_call | solution.py:330
  93.6 0.0 copy-done
  93.6 0.0 copy-done.2
  93.6 0.2 fusion
  93.8 0.0 copy-done.1
  93.8 1.8 %multiply_add_fusion = f32[1,256,256]{2,1,0:T(8,128)} fusion(f32[1,256,256]{2,1,0:T(8,128)} %fused.1, bf16[1,256,256]{2,1,0:T(8,128)(2,1)S(1)} %copy-done.1, f32[256]{0:T(256)S(1)} %bitcast.6), kind=kLoop, calls=%fused_computation | loop fusion | flops 196608 | bytes 656384 | tf_op jit(solution)/shard_map/add | solution.py:410
Async XLA Ops:
  0.0 93.6 %copy-start = (f32[16]{0:T(128)S(1)}, f32[16]{0:T(128)}, u32[]{:S(2)}) copy-start(f32[16]{0:T(128)} %param.14) | copy-start | bytes 196
  0.0 93.8 %copy-start.1 = (bf16[1,256,256]{2,1,0:T(8,128)(2,1)S(1)}, bf16[1,256,256]{2,1,0:T(8,128)(2,1)}, u32[]{:S(2)}) copy-start(bf16[1,256,256]{2,1,0:T(8,128)(2,1)} %probes_ref.1) | copy-start | bytes 393220
  0.0 93.6 %copy-start.2 = (s32[256]{0:T(256)S(1)}, s32[256]{0:T(256)}, u32[]{:S(2)}) copy-start(s32[256]{0:T(256)} %param.13) | copy-start | bytes 3076

commit v3 on v2

--- a/solution.py
+++ b/solution.py
@@ -12,6 +12,8 @@
 
 GROUP = 16
 HALVES = 2
+DEPTH = 8
+LANES = 128
 MESH = pl.DeviceIdType.MESH
 NT = (((1,), (1,)), ((), ()))
 TN = (((0,), (0,)), ((), ()))
@@ -44,13 +46,17 @@
     halves,
     k_hbm,
     probes_ref,
-    weight_ref,
+    mask_ref,
+    precision_ref,
+    block_ref,
+    damping_ref,
     fwd_t_ref,
     inv_ref,
     pick_ref,
     out_ref,
     stage,
-    kt_ref,
+    kt_first,
+    kt_last,
     gath,
     x_ref,
     et_ref,
@@ -79,9 +85,10 @@
     nown = nprobe // n_col
     groups = freqs // GROUP
     columns = nprobe * 2 * GROUP
-    rows = stage.shape[2]
+    depth, _, rows, _, _ = stage.shape
     steps = sensors // rows
     half = sensors // halves
+    kts = [kt_first, kt_last]
 
     def row_peer(d):
         return lax.rem(me_row + d, n_row)
@@ -93,7 +100,7 @@
         at = pl.ds(pl.multiple_of(step * rows, rows), rows)
         return pltpu.make_async_copy(k_hbm.at[:, at], stage.at[slot], k_sem.at[slot])
 
-    for slot in range(2):
+    for slot in range(depth):
         load(slot, slot).start()
 
     barrier = pltpu.get_barrier_semaphore()
@@ -125,26 +132,24 @@
         copy.start()
         gathers.append(copy)
 
-    def turn_step(step, carry):
-        slot = lax.rem(step, 2)
+    def turn(kt, slot, r, row):
+        for k in range(2):
+            kt[:, k, row, :, :] = stage[slot, k, r].T.reshape(groups, GROUP, sources)
+
+    def load_next(step, slot):
+        @pl.when(step + depth < steps)
+        def _():
+            load(step + depth, slot).start()
+
+    def turn_first(step, carry):
+        slot = lax.rem(step, depth)
         load(step, slot).wait()
-
-        def turn(r, inner):
-            for k in range(2):
-                kt_ref[:, k, step * rows + r, :, :] = stage[slot, k, r].T.reshape(
-                    groups, GROUP, sources
-                )
-            return inner
-
-        lax.fori_loop(0, rows, turn, 0, unroll=2)
-
-        @pl.when(step + 2 < steps)
-        def _():
-            load(step + 2, slot).start()
-
+        for r in range(rows):
+            turn(kt_first, slot, r, step * rows + r)
+        load_next(step, slot)
         return carry
 
-    lax.fori_loop(0, steps, turn_step, 0)
+    lax.fori_loop(0, groups, turn_first, 0)
 
     def spectra(p, block):
         spec = dot(fwd_t_ref[...], block, NT).astype(jnp.bfloat16)
@@ -165,6 +170,16 @@
         for j in range(nloc):
             spectra(origin * nloc + j, gath[d, j])
 
+    def column(row, width):
+        tall = jnp.broadcast_to(row, (LANES, row.shape[1])).T
+        return jnp.concatenate([tall] * (width // LANES), axis=1)
+
+    times = probes_ref.shape[2]
+    precision = precision_ref[...]
+    sensor_weight = column(
+        jnp.where(mask_ref[...] == 1, precision, jnp.zeros_like(precision)), times
+    )
+
     own = lax.broadcasted_iota(jnp.int32, (1, GROUP, columns), 1)
     col = lax.broadcasted_iota(jnp.int32, (1, GROUP, columns), 2) % GROUP
     keep = own == col
@@ -172,21 +187,37 @@
     col = lax.broadcasted_iota(jnp.int32, (1, GROUP, half * GROUP), 2) % GROUP
     keep_wide = own == col
 
+    def forward_chunk(h, g, first, count):
+        left = [
+            kts[h][g, k, first : first + count].reshape(count * GROUP, sources) for k in range(2)
+        ]
+        out = dot(left[0], x_ref[g, 0], NT) + dot(left[1], x_ref[g, 1], NT)
+        kept = jnp.where(keep, out.reshape(count, GROUP, columns), 0.0).astype(jnp.bfloat16)
+        return dot(pick_ref[:count, : count * GROUP], kept.reshape(count * GROUP, columns))
+
+    def store_blocks(g, block):
+        et_ref[:, :, g] = block.T.astype(jnp.bfloat16).reshape(nprobe, 2, GROUP, half)
+
+    def forward_turning(g, carry):
+        step = groups + g
+        slot = lax.rem(step, depth)
+        load(step, slot).wait()
+        count = half // 2
+        blocks = []
+        for piece in range(2):
+            for r in range(piece * rows // 2, (piece + 1) * rows // 2):
+                turn(kt_last, slot, r, g * rows + r)
+            blocks.append(forward_chunk(0, g, piece * count, count))
+        store_blocks(g, jnp.concatenate(blocks, axis=0))
+        load_next(step, slot)
+        return carry
+
     def forward_part(h, low, high):
         def one(g, carry):
-            left = [
-                kt_ref[g, k, h * half : (h + 1) * half].reshape(half * GROUP, sources)
-                for k in range(2)
-            ]
-            out = dot(left[0], x_ref[g, 0], NT) + dot(left[1], x_ref[g, 1], NT)
-            kept = jnp.where(keep, out.reshape(half, GROUP, columns), 0.0).astype(jnp.bfloat16)
-            block = dot(pick_ref[...], kept.reshape(half * GROUP, columns))
-            et_ref[:, :, g] = (
-                block.T.astype(jnp.bfloat16).reshape(nprobe, 2, GROUP, half)
-            )
+            store_blocks(g, forward_chunk(h, g, 0, half))
             return carry
 
-        lax.fori_loop(low, high, one, 0)
+        lax.fori_loop(low, high, one, 0, unroll=2)
 
     sends = []
 
@@ -213,7 +244,7 @@
         for d in range(1, n_col):
             copies[d - 1].wait_recv()
             total = total + pred_in[h, d - 1].astype(jnp.float32)
-        scale = weight_ref[h * half : (h + 1) * half, :]
+        scale = sensor_weight[h * half : (h + 1) * half]
         wt_ref[h, me_col] = (total * scale[None]).astype(jnp.bfloat16)
         out = []
         for d in range(1, n_col):
@@ -247,7 +278,7 @@
             wide = wide.reshape(columns, half * GROUP)
             both = [
                 dot(
-                    wide, kt_ref[g, k, h * half : (h + 1) * half].reshape(half * GROUP, sources)
+                    wide, kts[h][g, k].reshape(half * GROUP, sources)
                 ).reshape(nprobe, 2, GROUP, sources)
                 for k in range(2)
             ]
@@ -264,10 +295,10 @@
                 g_ref[:, 1, g] = imag.astype(jnp.bfloat16)
             return carry
 
-        lax.fori_loop(low, high, one, 0)
+        lax.fori_loop(low, high, one, 0, unroll=2)
 
     mid = groups // 2
-    forward_part(0, 0, groups)
+    lax.fori_loop(0, groups, forward_turning, 0)
     pred_copies = predict(0)
     for h in range(1, halves):
         forward_part(h, 0, mid)
@@ -278,8 +309,6 @@
         adjoint_part(h - 1, 0, mid)
         wt_copies = weigh(h, pred_copies)
         adjoint_part(h - 1, mid, groups)
-    if halves == 1:
-        wt_copies = weigh(0, pred_copies)
     residual(halves - 1, wt_copies)
     adjoint_part(halves - 1, 0, groups)
 
@@ -300,9 +329,14 @@
         )
         copy.start()
         backs.append(copy)
+    group_of = block_ref[...]
+    damp = jnp.zeros(group_of.shape, jnp.float32)
+    for n in range(damping_ref.shape[0]):
+        damp = jnp.where(group_of == n, damping_ref[n], damp)
+    damp = column(damp, times)
     for j in range(nloc):
         total = history(me_row * nloc + j).astype(jnp.float32)
-        out_ref[j] = total
+        out_ref[j] = total + damp * probes_ref[j].astype(jnp.float32)
     for d in range(1, n_row):
         backs[d - 1].wait_recv()
         for j in range(nloc):
@@ -311,7 +345,17 @@
         copy.wait_send()
 
 
-def fused_call(mesh_sizes, kernel_spectra, probes, weight, fwd_t, inverse):
+def fused_call(
+    mesh_sizes,
+    kernel_spectra,
+    probes,
+    sensor_mask,
+    precision,
+    source_block,
+    damping,
+    fwd_t,
+    inverse,
+):
     n_row, n_col = mesh_sizes
     _, sensors, sources, freqs = kernel_spectra.shape
     nloc, _, times = probes.shape
@@ -321,7 +365,7 @@
     columns = nprobe * 2 * GROUP
     halves = HALVES
     half = sensors // halves
-    rows = 16
+    rows = half // groups
     owner = np.arange(half * GROUP)[None, :] // GROUP
     pick = jnp.asarray((np.arange(half)[:, None] == owner).astype(ml_dtypes.bfloat16))
     vmem = pl.BlockSpec(memory_space=pltpu.VMEM)
@@ -329,12 +373,16 @@
     dma = pltpu.SemaphoreType.DMA
     return pl.pallas_call(
         functools.partial(fused_kernel, n_row, n_col, halves),
-        in_specs=[pl.BlockSpec(memory_space=pl.ANY)] + [vmem] * 5,
+        in_specs=[pl.BlockSpec(memory_space=pl.ANY)]
+        + [vmem] * 4
+        + [pl.BlockSpec(memory_space=pltpu.SMEM)]
+        + [vmem] * 3,
         out_specs=vmem,
         out_shape=jax.ShapeDtypeStruct(probes.shape, jnp.float32),
         scratch_shapes=[
-            pltpu.VMEM((2, 2, rows, sources, freqs), low),
-            pltpu.VMEM((groups, 2, sensors, GROUP, sources), low),
+            pltpu.VMEM((DEPTH, 2, rows, sources, freqs), low),
+            pltpu.VMEM((groups, 2, half, GROUP, sources), low),
+            pltpu.VMEM((groups, 2, half, GROUP, sources), low),
             pltpu.VMEM((n_row,) + probes.shape, low),
             pltpu.VMEM((groups, 2, columns, sources), low),
             pltpu.VMEM((nprobe, 2, groups, GROUP, half), low),
@@ -346,7 +394,7 @@
             pltpu.VMEM((nprobe, 2, groups, GROUP, sources), low),
             pltpu.VMEM((n_row - 1,) + probes.shape, low),
             pltpu.VMEM((n_row - 1,) + probes.shape, low),
-            dma((2,)),
+            dma((DEPTH,)),
             dma((n_row,)),
             dma((n_row,)),
             dma((halves, n_col - 1)),
@@ -360,7 +408,17 @@
             vmem_limit_bytes=60 * 1024 * 1024, collective_id=0, has_side_effects=True
         ),
         name="fused",
-    )(kernel_spectra, probes, weight, fwd_t, inverse, pick)
+    )(
+        kernel_spectra,
+        probes,
+        sensor_mask[None, :],
+        precision[None, :],
+        source_block[None, :],
+        damping,
+        fwd_t,
+        inverse,
+        pick,
+    )
 
 
 def plain_forward(kernel_spectra, probes, fwd_t, inv_t):
@@ -399,13 +457,24 @@
     forward, inverse = dft_tables(probes.shape[2])
     fwd_t, inverse = jnp.asarray(forward.T), jnp.asarray(inverse)
     _, sensors, sources, freqs = kernel_spectra.shape
+    half, groups = sensors // HALVES, freqs // GROUP
+    aligned = all(size % LANES == 0 for size in (sensors, sources, freqs))
+    if aligned and half % (2 * groups) == 0 and sensors // (half // groups) >= DEPTH:
+        return fused_call(
+            sizes,
+            kernel_spectra,
+            probes,
+            sensor_mask,
+            precision,
+            source_block,
+            damping,
+            fwd_t,
+            inverse,
+        )
     record_weight = jnp.where(sensor_mask == 1, precision, jnp.zeros_like(precision))
-    if sensors % 128 == 0 and sources % 128 == 0 and freqs % 128 == 0:
-        summed = fused_call(sizes, kernel_spectra, probes, record_weight[:, None], fwd_t, inverse)
-    else:
-        summed = plain(kernel_spectra, probes, record_weight, fwd_t, inverse)
-    groups = jnp.arange(damping.shape[0], dtype=jnp.int32)
-    one_hot = (source_block[:, None] == groups[None, :]).astype(jnp.float32)
+    summed = plain(kernel_spectra, probes, record_weight, fwd_t, inverse)
+    numbers = jnp.arange(damping.shape[0], dtype=jnp.int32)
+    one_hot = (source_block[:, None] == numbers[None, :]).astype(jnp.float32)
     source_damping = jnp.dot(one_hot, damping, precision=lax.Precision.HIGHEST)
     return summed + source_damping[None, :, None] * probes.astype(jnp.float32)
 

time: 96 us -> 89.7 us (0.934)
  Pallas kernels: 92.1 us -> 87.9 us
  other arithmetic: 2.55 us -> 0 us
    pallas_call x1, Pallas kernels: 92.1 us -> 87.9 us  [fused_call(): pl.pallas_call(functools.partial(fused_kernel, n_row, n_col, halves), in_...]
    add x1 -> x0, other arithmetic: 1.83 us -> none  [body(): return summed + source_damping[None, :, None] * probes.astype(jnp.float32)]
    unnamed x6 -> x1, local copies, waits for them, and re-layouts: 0.01 us -> 1.67 us
where the time goes in v3:
time: 89.7 us; the launch traced here: 89.5 us
  Pallas kernels  87.9 us (98%)
  local copies, waits for them, and re-layouts  1.67 us (2%)
    pallas_call x1, Pallas kernels, fused_call(): pl.pallas_call(functools.partial(fused_kernel, n_row, n_col, halves), in_...  87.9 us

profile of v3, /device:TPU:1, one launch (start us, length us, event | category | flops | bytes accessed | tf_op | source)
XLA Modules:
  0.0 89.5 jit_solution(15621381777422037303)
XLA Ops:
  0.0 87.9 %fused.1 = f32[1,256,256]{2,1,0:T(8,128)} custom-call(bf16[2,128,256,256]{3,2,1,0:T(8,128)(2,1)} %k_hbm.1, bf16[1,256,256]{2,1,0:T(8,128)(2,1)} %probes_ref.1, s32[1,128]{1,0:T(1,128)} %bitcast.4, f32[1,128]{1,0:T(1,128)} %bitcast.5, s32[1,256]{1,0:T(1,128)} %bitcast.3, f32[16]{0:T(128)} %damping_ref.1, bf16[512,256]{1,0:T(8,128)(2,1)} %constant.6.clone.fwd_t_ref, ...), custom_call_target="tpu_custom_call" | custom-call | tf_op jit(solution)/shard_map/fused/pallas_call | solution.py:374
  87.9 1.7 %copy.11 = f32[1,256,256]{2,1,0:T(8,128)} copy(f32[1,256,256]{2,1,0:T(8,128)} %fused.1) | data formatting | bytes 524288

commit v4 on v3

--- a/solution.py
+++ b/solution.py
@@ -66,8 +66,12 @@
     y_ref,
     acc_ref,
     g_ref,
-    hess_out,
-    hess_in,
+    wide_even,
+    wide_odd,
+    pair_out,
+    pair_in,
+    far_out,
+    far_in,
     k_sem,
     gs_sem,
     gr_sem,
@@ -77,6 +81,8 @@
     wr_sem,
     hs_sem,
     hr_sem,
+    fs_sem,
+    fr_sem,
 ):
     me_row, me_col = lax.axis_index("row"), lax.axis_index("col")
     _, sensors, sources, freqs = k_hbm.shape
@@ -157,10 +163,10 @@
         imag = spec[freqs:].reshape(groups, GROUP, sources)
         first = pl.ds(pl.multiple_of(p * 2 * GROUP, GROUP), GROUP)
         second = pl.ds(pl.multiple_of(p * 2 * GROUP + GROUP, GROUP), GROUP)
-        x_ref[:, 0, first, :] = real
-        x_ref[:, 0, second, :] = imag
-        x_ref[:, 1, first, :] = -imag
-        x_ref[:, 1, second, :] = real
+        x_ref[:, first, :sources] = real
+        x_ref[:, second, :sources] = imag
+        x_ref[:, first, sources:] = -imag
+        x_ref[:, second, sources:] = real
 
     for j in range(nloc):
         spectra(me_row * nloc + j, probes_ref[j])
@@ -191,7 +197,7 @@
         left = [
             kts[h][g, k, first : first + count].reshape(count * GROUP, sources) for k in range(2)
         ]
-        out = dot(left[0], x_ref[g, 0], NT) + dot(left[1], x_ref[g, 1], NT)
+        out = dot(jnp.concatenate(left, axis=1), x_ref[g], NT)
         kept = jnp.where(keep, out.reshape(count, GROUP, columns), 0.0).astype(jnp.bfloat16)
         return dot(pick_ref[:count, : count * GROUP], kept.reshape(count * GROUP, columns))
 
@@ -271,31 +277,42 @@
                     groups, GROUP, half
                 )
 
+    def widen(g, wide_ref):
+        wide = dot(y_ref[g], pick_ref[...]).reshape(2 * nprobe, GROUP, half * GROUP)
+        wide = jnp.where(keep_wide, wide, 0.0).astype(jnp.bfloat16)
+        wide_ref[...] = wide.reshape(columns, half * GROUP)
+
+    def multiply(h, g, wide_ref):
+        both = [
+            dot(wide_ref[...], kts[h][g, k].reshape(half * GROUP, sources)).reshape(
+                nprobe, 2, GROUP, sources
+            )
+            for k in range(2)
+        ]
+        real = both[0][:, 0] + both[1][:, 1]
+        imag = both[0][:, 1] - both[1][:, 0]
+        if h > 0:
+            real = real + acc_ref[g, 0]
+            imag = imag + acc_ref[g, 1]
+        if h < halves - 1:
+            acc_ref[g, 0] = real
+            acc_ref[g, 1] = imag
+        else:
+            g_ref[:, 0, g] = real.astype(jnp.bfloat16)
+            g_ref[:, 1, g] = imag.astype(jnp.bfloat16)
+
     def adjoint_part(h, low, high):
-        def one(g, carry):
-            wide = dot(y_ref[g], pick_ref[...]).reshape(2 * nprobe, GROUP, half * GROUP)
-            wide = jnp.where(keep_wide, wide, 0.0).astype(jnp.bfloat16)
-            wide = wide.reshape(columns, half * GROUP)
-            both = [
-                dot(
-                    wide, kts[h][g, k].reshape(half * GROUP, sources)
-                ).reshape(nprobe, 2, GROUP, sources)
-                for k in range(2)
-            ]
-            real = both[0][:, 0] + both[1][:, 1]
-            imag = both[0][:, 1] - both[1][:, 0]
-            if h > 0:
-                real = real + acc_ref[g, 0]
-                imag = imag + acc_ref[g, 1]
-            if h < halves - 1:
-                acc_ref[g, 0] = real
-                acc_ref[g, 1] = imag
-            else:
-                g_ref[:, 0, g] = real.astype(jnp.bfloat16)
-                g_ref[:, 1, g] = imag.astype(jnp.bfloat16)
+        widen(low, wide_even)
+
+        def two(i, carry):
+            g = low + 2 * i
+            widen(g + 1, wide_odd)
+            multiply(h, g, wide_even)
+            widen(lax.rem(g + 2, groups), wide_even)
+            multiply(h, g + 1, wide_odd)
             return carry
 
-        lax.fori_loop(low, high, one, 0, unroll=2)
+        lax.fori_loop(0, (high - low) // 2, two, 0)
 
     mid = groups // 2
     lax.fori_loop(0, groups, forward_turning, 0)
@@ -313,35 +330,51 @@
     adjoint_part(halves - 1, 0, groups)
 
     def history(p):
-        return dot(g_ref[p].reshape(2 * freqs, sources), fwd_t_ref[...], TN).astype(jnp.bfloat16)
-
-    backs = []
-    for d in range(1, n_row):
-        peer = row_peer(d)
+        return dot(g_ref[p].reshape(2 * freqs, sources), fwd_t_ref[...], TN)
+
+    def flip(change):
+        place, bit = 0, 1
+        while bit < n_row:
+            place = place + lax.rem(lax.div(me_row, bit) + (change // bit) % 2, 2) * bit
+            bit *= 2
+        return place
+
+    changes = list(range(n_row - 2, -1, -2))
+    backs, joins = [], []
+    for i, change in enumerate(changes):
+        peer = flip(change + 1)
         for j in range(nloc):
-            hess_out[d - 1, j] = history(peer * nloc + j)
+            pair_out[i, j] = history(peer * nloc + j).astype(jnp.bfloat16)
         copy = send(
-            hess_out.at[d - 1],
-            hess_in.at[d - 1],
-            hs_sem.at[d - 1],
-            hr_sem.at[d - 1],
-            (peer, me_col),
+            pair_out.at[i], pair_in.at[i], hs_sem.at[i], hr_sem.at[i], (flip(1), me_col)
         )
         copy.start()
-        backs.append(copy)
+        joins.append(copy)
+    for i, change in enumerate(changes):
+        peer = flip(change)
+        total = [history(peer * nloc + j) for j in range(nloc)]
+        joins[i].wait_recv()
+        total = [total[j] + pair_in[i, j].astype(jnp.float32) for j in range(nloc)]
+        if change > 0:
+            for j in range(nloc):
+                far_out[i, j] = total[j].astype(jnp.bfloat16)
+            copy = send(
+                far_out.at[i], far_in.at[i], fs_sem.at[i], fr_sem.at[i], (peer, me_col)
+            )
+            copy.start()
+            backs.append(copy)
     group_of = block_ref[...]
     damp = jnp.zeros(group_of.shape, jnp.float32)
     for n in range(damping_ref.shape[0]):
         damp = jnp.where(group_of == n, damping_ref[n], damp)
     damp = column(damp, times)
     for j in range(nloc):
-        total = history(me_row * nloc + j).astype(jnp.float32)
-        out_ref[j] = total + damp * probes_ref[j].astype(jnp.float32)
-    for d in range(1, n_row):
-        backs[d - 1].wait_recv()
+        out_ref[j] = total[j] + damp * probes_ref[j].astype(jnp.float32)
+    for i, copy in enumerate(backs):
+        copy.wait_recv()
         for j in range(nloc):
-            out_ref[j] += hess_in[d - 1, j].astype(jnp.float32)
-    for copy in gathers + sends + backs:
+            out_ref[j] += far_in[i, j].astype(jnp.float32)
+    for copy in gathers + sends + joins + backs:
         copy.wait_send()
 
 
@@ -384,7 +417,7 @@
             pltpu.VMEM((groups, 2, half, GROUP, sources), low),
             pltpu.VMEM((groups, 2, half, GROUP, sources), low),
             pltpu.VMEM((n_row,) + probes.shape, low),
-            pltpu.VMEM((groups, 2, columns, sources), low),
+            pltpu.VMEM((groups, columns, 2 * sources), low),
             pltpu.VMEM((nprobe, 2, groups, GROUP, half), low),
             pltpu.VMEM((halves, n_col, nown, half, times), low),
             pltpu.VMEM((halves, n_col - 1, nown, half, times), low),
@@ -392,8 +425,12 @@
             pltpu.VMEM((groups, columns, half), low),
             pltpu.VMEM((groups, 2, nprobe, GROUP, sources), jnp.float32),
             pltpu.VMEM((nprobe, 2, groups, GROUP, sources), low),
-            pltpu.VMEM((n_row - 1,) + probes.shape, low),
-            pltpu.VMEM((n_row - 1,) + probes.shape, low),
+            pltpu.VMEM((columns, half * GROUP), low),
+            pltpu.VMEM((columns, half * GROUP), low),
+            pltpu.VMEM((n_row // 2,) + probes.shape, low),
+            pltpu.VMEM((n_row // 2,) + probes.shape, low),
+            pltpu.VMEM((n_row // 2 - 1,) + probes.shape, low),
+            pltpu.VMEM((n_row // 2 - 1,) + probes.shape, low),
             dma((DEPTH,)),
             dma((n_row,)),
             dma((n_row,)),
@@ -401,8 +438,10 @@
             dma((halves, n_col - 1)),
             dma((halves, n_col - 1)),
             dma((halves, n_col - 1)),
-            dma((n_row - 1,)),
-            dma((n_row - 1,)),
+            dma((n_row // 2,)),
+            dma((n_row // 2,)),
+            dma((n_row // 2 - 1,)),
+            dma((n_row // 2 - 1,)),
         ],
         compiler_params=pltpu.CompilerParams(
             vmem_limit_bytes=60 * 1024 * 1024, collective_id=0, has_side_effects=True
@@ -459,7 +498,8 @@
     _, sensors, sources, freqs = kernel_spectra.shape
     half, groups = sensors // HALVES, freqs // GROUP
     aligned = all(size % LANES == 0 for size in (sensors, sources, freqs))
-    if aligned and half % (2 * groups) == 0 and sensors // (half // groups) >= DEPTH:
+    paired = sizes[0] >= 4 and sizes[0] & (sizes[0] - 1) == 0
+    if aligned and paired and half % (2 * groups) == 0 and sensors // (half // groups) >= DEPTH:
         return fused_call(
             sizes,
             kernel_spectra,

time: 89.7 us -> 87 us (0.970)
  Pallas kernels: 87.9 us -> 84.6 us
    pallas_call x1, Pallas kernels: 87.9 us -> 84.6 us  [fused_call(): pl.pallas_call(functools.partial(fused_kernel, n_row, n_col, halves), in_...]
where the time goes in v4:
time: 87 us; the launch traced here: 86.3 us
  Pallas kernels  84.6 us (97%)
  local copies, waits for them, and re-layouts  1.67 us (2%)
    pallas_call x1, Pallas kernels, fused_call(): pl.pallas_call(functools.partial(fused_kernel, n_row, n_col, halves), in_...  84.6 us

profile of v4, /device:TPU:1, one launch (start us, length us, event | category | flops | bytes accessed | tf_op | source)
XLA Modules:
  0.0 86.3 jit_solution(13248075511706111728)
XLA Ops:
  0.0 84.6 %fused.1 = f32[1,256,256]{2,1,0:T(8,128)} custom-call(bf16[2,128,256,256]{3,2,1,0:T(8,128)(2,1)} %k_hbm.1, bf16[1,256,256]{2,1,0:T(8,128)(2,1)} %probes_ref.1, s32[1,128]{1,0:T(1,128)} %bitcast.4, f32[1,128]{1,0:T(1,128)} %bitcast.5, s32[1,256]{1,0:T(1,128)} %bitcast.3, f32[16]{0:T(128)} %damping_ref.1, bf16[512,256]{1,0:T(8,128)(2,1)} %constant.6.clone.fwd_t_ref, ...), custom_call_target="tpu_custom_call" | custom-call | tf_op jit(solution)/shard_map/fused/pallas_call | solution.py:407
  84.6 1.7 %copy.11 = f32[1,256,256]{2,1,0:T(8,128)} copy(f32[1,256,256]{2,1,0:T(8,128)} %fused.1) | data formatting | bytes 524288

commit v5 on v4

--- a/solution.py
+++ b/solution.py
@@ -53,6 +53,7 @@
     fwd_t_ref,
     inv_ref,
     pick_ref,
+    eye_ref,
     out_ref,
     stage,
     kt_first,
@@ -139,8 +140,10 @@
         gathers.append(copy)
 
     def turn(kt, slot, r, row):
-        for k in range(2):
-            kt[:, k, row, :, :] = stage[slot, k, r].T.reshape(groups, GROUP, sources)
+        real = stage[slot, 0, r].T
+        imag = dot(eye_ref[...], stage[slot, 1, r], NT).astype(jnp.bfloat16)
+        kt[:, 0, row, :, :] = real.reshape(groups, GROUP, sources)
+        kt[:, 1, row, :, :] = imag.reshape(groups, GROUP, sources)
 
     def load_next(step, slot):
         @pl.when(step + depth < steps)
@@ -409,7 +412,7 @@
         in_specs=[pl.BlockSpec(memory_space=pl.ANY)]
         + [vmem] * 4
         + [pl.BlockSpec(memory_space=pltpu.SMEM)]
-        + [vmem] * 3,
+        + [vmem] * 4,
         out_specs=vmem,
         out_shape=jax.ShapeDtypeStruct(probes.shape, jnp.float32),
         scratch_shapes=[
@@ -457,6 +460,7 @@
         fwd_t,
         inverse,
         pick,
+        jnp.asarray(np.eye(freqs).astype(ml_dtypes.bfloat16)),
     )
 
 

time: 87 us -> 91.4 us (1.051)
  Pallas kernels: 84.6 us -> 89 us
    pallas_call x1, Pallas kernels: 84.6 us -> 89 us  [fused_call(): pl.pallas_call(functools.partial(fused_kernel, n_row, n_col, halves), in_...]
where the time goes in v5:
time: 91.4 us; the launch traced here: 90.6 us
  Pallas kernels  89 us (97%)
  local copies, waits for them, and re-layouts  1.67 us (2%)
    pallas_call x1, Pallas kernels, fused_call(): pl.pallas_call(functools.partial(fused_kernel, n_row, n_col, halves), in_...  89 us

profile of v5, /device:TPU:1, one launch (start us, length us, event | category | flops | bytes accessed | tf_op | source)
XLA Modules:
  0.0 90.6 jit_solution(7375512272940538029)
XLA Ops:
  0.0 89.0 %fused.1 = f32[1,256,256]{2,1,0:T(8,128)} custom-call(bf16[2,128,256,256]{3,2,1,0:T(8,128)(2,1)} %k_hbm.1, bf16[1,256,256]{2,1,0:T(8,128)(2,1)} %probes_ref.1, s32[1,128]{1,0:T(1,128)} %bitcast.4, f32[1,128]{1,0:T(1,128)} %bitcast.5, s32[1,256]{1,0:T(1,128)} %bitcast.3, f32[16]{0:T(128)} %damping_ref.1, bf16[512,256]{1,0:T(8,128)(2,1)} %constant.8.clone.fwd_t_ref, ...), custom_call_target="tpu_custom_call" | custom-call | tf_op jit(solution)/shard_map/fused/pallas_call | solution.py:410
  89.0 1.7 %copy.12 = f32[1,256,256]{2,1,0:T(8,128)} copy(f32[1,256,256]{2,1,0:T(8,128)} %fused.1) | data formatting | bytes 524288
